TPU v7x, 512 devices: a whole 4x8x8 slice. The times are simulated.
512 devices in a mesh: expert: 128 (over z, y, core), dp: 4 (over x).
Axes of the slice: x: 4, y: 8, z: 8, core: 2. Of those that a mesh axis runs over, the one named last changes fastest.
Arguments:
- tokens: bfloat16 [256, 4096], P('expert', 'dp'), may hold values from -6 to 6
- routing: int32 [256, 8], P('expert'), may hold values from 0 to 31, all different within a row; in each aligned block of 2 rows (0 to 1, 2 to 3, ...) at most 2 rows name the same one
- combine_weights: float32 [256, 8], P('expert'), may hold values from 0.05 to 0.4
- gate_weight: bfloat16 [49152, 4096], P('expert', 'dp'), may hold values from -0.09375 to 0.09375
- up_weight: bfloat16 [49152, 4096], P('expert', 'dp'), may hold values from -0.09375 to 0.09375
- down_weight: bfloat16 [49152, 4096], P('expert', 'dp'), may hold values from -0.15625 to 0.15625
Outputs:
- layer_output: bfloat16 [256, 4096], P('expert', 'dp')
Inputs may be any that keep to these rules, and one draw needn't show every extreme that they name: `routing`: each row names 8 different experts. Among the 2 rows of one index of the expert axis, no expert is named by more than 2 rows, and in some of these blocks one expert is named by exactly 2.
All inputs are finite; a program needn't handle non-finite values.
Results may differ from a plain program's by a relative error of at most 0.025.
Values may be sent and summed in bfloat16 or wider, within the bound.
A program may use at most 64 MiB of HBM per device.

v0:
```python
import jax
import jax.numpy as jnp
from jax import lax
from jax.sharding import PartitionSpec as P

FF = 1536


def contract_last(left_side, right_side):
    return lax.dot_general(
        left_side, right_side, (((1,), (1,)), ((), ())), preferred_element_type=jnp.float32
    )


def activate(linear_both, hidden_units):
    pre_gate = linear_both[:, :hidden_units]
    pre_up = linear_both[:, hidden_units:]
    return (jax.nn.sigmoid(pre_gate) * pre_gate * pre_up).astype(jnp.bfloat16)


def shards(tokens, routing, combine_weights, gate_weight, up_weight, down_weight):
    members = lax.axis_size("expert")
    local_tokens = tokens.shape[0]
    features = tokens.shape[1]
    hidden_units = gate_weight.shape[0]
    slices = FF // hidden_units
    expert_count = members // slices
    numbers = jnp.arange(expert_count, dtype=jnp.int32)
    picked = routing[None, :, :] == numbers[:, None, None]
    chosen = jnp.any(picked, axis=2)
    weight = jnp.sum(jnp.where(picked, combine_weights[None, :, :], 0.0), axis=2)
    places = jnp.arange(local_tokens, dtype=jnp.int32)
    diagonal = places[:, None] == jnp.arange(local_tokens, dtype=jnp.int32)[None, :]
    layout = chosen[:, None, :] & diagonal[None, :, :]
    mapping = layout.astype(jnp.bfloat16)
    token_send = jnp.einsum(
        "ecj,jd->ecd", mapping, tokens, preferred_element_type=jnp.float32
    ).astype(jnp.bfloat16)
    token_send = jnp.repeat(token_send, slices, axis=0)
    token_recv = lax.all_to_all(token_send, "expert", split_axis=0, concat_axis=0, tiled=True)
    row_count = members * local_tokens
    token_rows = token_recv.reshape(row_count, features)
    stacked = jnp.concatenate([gate_weight, up_weight], axis=0)
    linear_part = contract_last(token_rows, stacked)
    linear_both = lax.psum(linear_part.astype(jnp.bfloat16), "dp").astype(jnp.float32)
    hidden = activate(linear_both, hidden_units)
    output_part = jnp.dot(hidden, down_weight, preferred_element_type=jnp.float32).astype(
        jnp.bfloat16
    )
    output_back = lax.all_to_all(
        output_part.reshape(members, local_tokens, features),
        "expert",
        split_axis=0,
        concat_axis=0,
        tiled=True,
    )
    output_back = output_back.reshape(expert_count, slices, local_tokens, features)
    expert_terms = jnp.einsum(
        "ecj,escd->ejd", mapping, output_back, preferred_element_type=jnp.float32
    )
    return jnp.sum(weight[:, :, None] * expert_terms, axis=0).astype(jnp.bfloat16)


def solution(mesh):
    return jax.shard_map(
        shards,
        mesh=mesh,
        in_specs=(
            P("expert", "dp"),
            P("expert", None),
            P("expert", None),
            P("expert", "dp"),
            P("expert", "dp"),
            P("expert", "dp"),
        ),
        out_specs=P("expert", "dp"),
        check_vma=False,
    )
```

profile of v0, /device:TPU:1, one launch (start us, length us, event | category | flops | bytes accessed | tf_op | source)
XLA Modules:
  0.0 141.9 jit_solution(8091889720075903474)
XLA Ops:
  6.5 0.8 fusion.11
  7.4 0.1 copy.10
  7.5 0.1 broadcast_and_fusion
  7.6 0.1 copy.11
  7.7 0.9 convolution_convert_fusion.1
  8.6 0.1 copy.12
  8.8 0.3 broadcast_in_dim.16
  9.1 0.0 copy-start.4
  9.1 38.9 %all_to_all.10 = bf16[128,2,1024]{2,1,0:T(2,128)(2,1)S(1)} all-to-all(bf16[128,2,1024]{2,1,0:T(2,128)(2,1)S(1)} %bitcast.11), channel_id=1, replica_groups=mesh['expert'=128,'dp'=4] {'expert'}, dimensions={0} | all-to-all | bytes 1048576 | tf_op jit(solution)/shard_map/all_to_all | solution.py:40
  48.0 0.2 reshape.29
  48.2 0.9 copy-done.3
  49.2 1.4 fusion.4
  50.5 0.0 all-reduce.2.cloned.1.call-update
  50.5 43.4 %all-reduce.2.cloned.1.call-done = bf16[256,768]{1,0:T(8,128)(2,1)} async-done(((bf16[256,768]{1,0:T(8,128)(2,1)}), bf16[256,768]{1,0:T(8,128)(2,1)}) %all-reduce.2.cloned.1.call-update) | async-done | bytes 393232 | tf_op jit(solution)/shard_map/psum | solution.py:45
  93.9 1.0 convert_element_type.27
  95.0 0.5 convolution_convert_fusion
  95.5 1.0 reshape.30
  96.5 16.6 %all-to-all-start.1 = ((bf16[128,2,1024]{2,1,0:T(2,128)(2,1)}), bf16[128,2,1024]{2,1,0:T(2,128)(2,1)S(1)}, u32[]{:S(2)}, u32[]{:S(2)}) async-start(bf16[128,2,1024]{2,1,0:T(2,128)(2,1)} %reshape.30), calls=%async_computation.1 | async-start | bytes 1048576 | tf_op jit(solution)/shard_map/all_to_all | solution.py:50
  113.0 0.0 copy-done.1
  113.0 0.1 select_reduce_fusion
  113.1 0.1 copy.9
  113.2 20.4 %all-to-all-done.1 = bf16[128,2,1024]{2,1,0:T(2,128)(2,1)S(1)} async-done(((bf16[128,2,1024]{2,1,0:T(2,128)(2,1)}), bf16[128,2,1024]{2,1,0:T(2,128)(2,1)S(1)}, u32[]{:S(2)}, u32[]{:S(2)}) %all-to-all-start.1) | async-done | bytes 524320 | tf_op jit(solution)/shard_map/all_to_all | solution.py:50
  133.6 0.5 convert_reduce_fusion
  134.1 1.0 fusion.7
  (9 shorter events, 0.0 us)
Async XLA Ops:
  6.5 88.5 %copy-start = (bf16[384,1024]{1,0:T(8,128)(2,1)S(1)}, bf16[384,1024]{1,0:T(8,128)(2,1)}, u32[]{:S(2)}) copy-start(bf16[384,1024]{1,0:T(8,128)(2,1)} %param.11) | copy-start | bytes 2359300
  6.5 87.4 %all-reduce.2.cloned.1.call-start = ((), (), s32[]{:S(2)}) async-start(), calls=%async_computation.2 | async-start | bytes 786432 | tf_op jit(solution)/shard_map/psum | solution.py:45
  9.1 39.1 %copy-start.4 = (bf16[384,1024]{1,0:T(8,128)(2,1)S(1)}, bf16[384,1024]{1,0:T(8,128)(2,1)}, u32[]{:S(2)}) copy-start(bf16[384,1024]{1,0:T(8,128)(2,1)} %param.9) | copy-start | bytes 2359300
  48.0 1.1 copy-start.3
  96.5 16.6 %copy-start.1 = (s32[2,8]{1,0:T(2,128)S(1)}, s32[2,8]{1,0:T(2,128)}, u32[]{:S(2)}) copy-start(s32[2,8]{1,0:T(2,128)} %param.7) | copy-start | bytes 196
  96.5 16.6 %copy-start.2 = (f32[2,8]{1,0:T(2,128)S(1)}, f32[2,8]{1,0:T(2,128)}, u32[]{:S(2)}) copy-start(f32[2,8]{1,0:T(2,128)} %param.8) | copy-start | bytes 196
  96.5 37.1 %all-to-all-start.1 = ((bf16[128,2,1024]{2,1,0:T(2,128)(2,1)}), bf16[128,2,1024]{2,1,0:T(2,128)(2,1)S(1)}, u32[]{:S(2)}, u32[]{:S(2)}) async-start(bf16[128,2,1024]{2,1,0:T(2,128)(2,1)} %reshape.30), calls=%async_computation.1 | async-start | bytes 1048576 | tf_op jit(solution)/shard_map/all_to_all | solution.py:50
Sparse Core Ops, SparseCore 0:
  50.7 43.2 all-reduce.1
where the time goes:
time: 142 us
  waiting for transfers between devices  63.8 us (45%)
  blocking collectives  38.9 us (27%)
  starting transfers between devices  16.6 us (12%)
  between operations  13.5 us (10%)
  matrix products  3.71 us (3%)
  local copies, waits for them, and re-layouts  2.85 us (2%)
  other arithmetic  2.59 us (2%)
    psum x1, waiting for transfers between devices, shards(): lax.psum(linear_part.astype(jnp.bfloat16), 'dp').astype(jnp.float32)  43.4 us
    all_to_all x1, blocking collectives, shards(): lax.all_to_all(token_send, 'expert', split_axis=0, concat_axis=0, tiled=T...  38.9 us
    all_to_all x1, waiting for transfers between devices, shards(): lax.all_to_all(output_part.reshape(members, local_tokens, features), 'exp...  20.4 us
    all_to_all x1, starting transfers between devices, shards(): lax.all_to_all(output_part.reshape(members, local_tokens, features), 'exp...  16.6 us
  transfers between devices with their start and end apart: 2, of which 2 were waited for; matrix products, arithmetic and copies ran while one was open for 0% of the time, Pallas kernels for 0%

commit v1 on v0

v1 whole, which is shorter than its diff:
```python
import jax
import jax.numpy as jnp
from jax import lax
from jax.experimental import pallas as pl
from jax.experimental.pallas import tpu as pltpu
from jax.sharding import PartitionSpec as P

MESH = pl.DeviceIdType.MESH
F32, BF16 = jnp.float32, jnp.bfloat16
LINE = 8
FAR = (4, 3, 5, 2, 6, 1, 7)
NEAR = (1, 7, 2, 6, 3, 5, 4)
DP = (2, 1, 3)
D, H, PAY = 1024, 384, 1152
TOK, BLK = 2, 16
SLICES = 4
EXPERTS = 32


def body(tokens, routing, combine, gate_hbm, up_hbm, down_hbm, out,
         gate, up, down, pay, rows1, stage, gath, part, rs, hid, own, away, other, red, rows2, tmp,
         wsem, s1, r1, s2, r2, s3, r3, s4, r4, s5, r5, s6, r6, s7, r7, s8, r8):
    me = lax.axis_index("expert")
    x = lax.axis_index("dp")
    c = lax.rem(me, 2)
    y = lax.rem(me // 2, LINE)
    z = me // (2 * LINE)
    e = me // SLICES

    def at(a, b):
        zz = lax.rem(z + a * (1 - c) + b * c, LINE)
        yy = lax.rem(y + a * c + b * (1 - c), LINE)
        return ((zz * LINE + yy) * 2 + c, x)

    partner = (me + 1 - 2 * c, x)

    def over(d):
        return (me, lax.rem(x + d, 4))

    def send(src, dst, ssem, rsem, to):
        cp = pltpu.make_async_remote_copy(
            src_ref=src, dst_ref=dst, send_sem=ssem, recv_sem=rsem, device_id=to, device_id_type=MESH)
        cp.start()
        return cp

    barrier = pltpu.get_barrier_semaphore()
    for d in FAR:
        pl.semaphore_signal(barrier, inc=1, device_id=at(d, 0), device_id_type=MESH)
        pl.semaphore_signal(barrier, inc=1, device_id=at(0, d), device_id_type=MESH)
    for d in DP:
        pl.semaphore_signal(barrier, inc=1, device_id=over(d), device_id_type=MESH)
    pl.semaphore_signal(barrier, inc=1, device_id=partner, device_id_type=MESH)

    loads = [pltpu.make_async_copy(src, dst, wsem.at[i])
             for i, (src, dst) in enumerate(((gate_hbm, gate), (up_hbm, up), (down_hbm, down)))]
    for cp in loads:
        cp.start()

    pay[:, :D] = tokens[...]
    lane = lax.broadcasted_iota(jnp.int32, (TOK, 128), 1)
    dense = jnp.zeros((TOK, 128), F32)
    for k in range(8):
        dense = dense + jnp.where(lax.rem(lane, EXPERTS) == routing[:, k:k + 1], combine[:, k:k + 1], 0.0)
    high = dense.astype(BF16).astype(F32)
    pay[:, D:] = jnp.where(lane < EXPERTS, high, jnp.where(lane < 2 * EXPERTS, dense - high, 0.0)).astype(BF16)
    pl.semaphore_wait(barrier, 18)

    c1 = {d: send(pay, rows1.at[d], s1.at[d], r1.at[d], at(d, 0)) for d in FAR}
    stage[0:TOK, :] = pay[...].astype(F32)
    for d in NEAR:
        c1[d].wait_recv()
        stage[TOK * d:TOK * d + TOK, :] = rows1[d].astype(F32)
    gath[0, 0] = stage[...].astype(BF16)

    c2 = {d: send(gath.at[0, 0], gath.at[0, d], s2.at[d], r2.at[d], at(0, d)) for d in FAR}
    c3 = {0: send(gath.at[0, 0], gath.at[1, 0], s3.at[0], r3.at[0], partner)}
    for d in NEAR:
        c2[d].wait_recv()
        c3[d] = send(gath.at[0, d], gath.at[1, d], s3.at[d], r3.at[d], partner)
    for cp in loads:
        cp.wait()

    def linear(h):
        rows = gath[h, :, :, :D].reshape(128, D)
        for i, w in enumerate((gate, up)):
            lin = lax.dot_general(rows, w[...], (((1,), (1,)), ((), ())), preferred_element_type=F32)
            part[h, :, :, i * H:(i + 1) * H] = lin.astype(BF16).reshape(4, 32, H)
        return {d: send(part.at[h, lax.rem(x + d, 4)], rs.at[h, d], s4.at[h, d], r4.at[h, d], over(d)) for d in DP}

    c4 = [linear(0)]
    for d in range(LINE):
        c3[d].wait_recv()
    c4.append(linear(1))

    lanes = lax.broadcasted_iota(jnp.int32, (32, 128), 1)
    mine = (lanes == e) | (lanes == e + EXPERTS)

    def activate(h):
        total = part[h, x].astype(F32)
        for d in (1, 3, 2):
            c4[h][d].wait_recv()
            total = total + rs[h, d].astype(F32)
        wrow = gath[h, pl.ds(2 * x, 2), :, D:].reshape(32, 128).astype(F32)
        weight = jnp.sum(jnp.where(mine, wrow, 0.0), axis=1, keepdims=True)
        g, u = total[:, :H], total[:, H:]
        hid[h, x] = (jax.nn.sigmoid(g) * g * u * weight).astype(BF16)
        return {d: send(hid.at[h, x], hid.at[h, x], s5.at[h, d], r5.at[h, d], over(d)) for d in DP}

    c5 = [activate(0), activate(1)]

    def product(h):
        for d in (1, 3, 2):
            c5[h][d].wait_recv()
        return jnp.dot(hid[h].reshape(128, H), down[...], preferred_element_type=F32)

    own[...] = product(0).reshape(LINE, BLK, D)
    away[...] = product(1).astype(BF16).reshape(LINE, BLK, D)

    order = FAR + (0,)
    c6 = {d: send(away.at[d], other.at[d], s6.at[d], r6.at[d], partner) for d in order}
    c7 = {}
    for d in order:
        c6[d].wait_recv()
        own[d] = own[d] + other[d].astype(F32)
        if d:
            tmp[d] = own[d].astype(BF16)
            c7[d] = send(tmp.at[d], red.at[d], s7.at[d], r7.at[d], at(0, LINE - d))
    total = own[0]
    for d in NEAR:
        c7[d].wait_recv()
        total = total + red[d].astype(F32)
    own[0] = total
    c8 = {}
    for d in FAR:
        rows2[0, d] = own[0, TOK * d:TOK * d + TOK, :].astype(BF16)
        c8[d] = send(rows2.at[0, d], rows2.at[1, d], s8.at[d], r8.at[d], at(LINE - d, 0))
    final = own[0, 0:TOK, :]
    for d in NEAR:
        c8[d].wait_recv()
        final = final + rows2[1, d].astype(F32)
    out[...] = final.astype(BF16)

    for group in (c1, c2, c3, c4[0], c4[1], c5[0], c5[1], c6, c7, c8):
        for cp in group.values():
            cp.wait_send()


def shards(tokens, routing, combine, gate, up, down):
    vmem = pl.BlockSpec(memory_space=pltpu.VMEM)
    hbm = pl.BlockSpec(memory_space=pl.ANY)
    dma = pltpu.SemaphoreType.DMA
    return pl.pallas_call(
        body,
        out_shape=jax.ShapeDtypeStruct((TOK, D), BF16),
        in_specs=[vmem, vmem, vmem, hbm, hbm, hbm],
        out_specs=vmem,
        scratch_shapes=[
            pltpu.VMEM((H, D), BF16), pltpu.VMEM((H, D), BF16), pltpu.VMEM((H, D), BF16),
            pltpu.VMEM((TOK, PAY), BF16),
            pltpu.VMEM((LINE, TOK, PAY), BF16),
            pltpu.VMEM((BLK, PAY), F32),
            pltpu.VMEM((2, LINE, BLK, PAY), BF16),
            pltpu.VMEM((2, 4, 32, 2 * H), BF16),
            pltpu.VMEM((2, 4, 32, 2 * H), BF16),
            pltpu.VMEM((2, 4, 32, H), BF16),
            pltpu.VMEM((LINE, BLK, D), F32),
            pltpu.VMEM((LINE, BLK, D), BF16),
            pltpu.VMEM((LINE, BLK, D), BF16),
            pltpu.VMEM((LINE, BLK, D), BF16),
            pltpu.VMEM((2, LINE, TOK, D), BF16),
            pltpu.VMEM((LINE, BLK, D), BF16),
            dma((3,)),
            dma((8,)), dma((8,)), dma((8,)), dma((8,)), dma((8,)), dma((8,)),
            dma((2, 4)), dma((2, 4)), dma((2, 4)), dma((2, 4)),
            dma((8,)), dma((8,)), dma((8,)), dma((8,)), dma((8,)), dma((8,)),
        ],
        compiler_params=pltpu.CompilerParams(
            collective_id=0, has_side_effects=True, vmem_limit_bytes=48 << 20),
        cost_estimate=pl.CostEstimate(flops=603979776, bytes_accessed=2400000, transcendentals=24576),
    )(tokens, routing, combine, gate, up, down)


def solution(mesh):
    return jax.shard_map(
        shards,
        mesh=mesh,
        in_specs=(
            P("expert", "dp"),
            P("expert", None),
            P("expert", None),
            P("expert", "dp"),
            P("expert", "dp"),
            P("expert", "dp"),
        ),
        out_specs=P("expert", "dp"),
        check_vma=False,
    )
```

time: 142 us -> 55.1 us (0.39)
  waiting for transfers between devices: 63.8 us -> 0 us
  Pallas kernels: 0 us -> 48.7 us
  blocking collectives: 38.9 us -> 0 us
  starting transfers between devices: 16.6 us -> 0 us
  between operations: 13.5 us -> 0.02 us
  matrix products: 3.71 us -> 0 us
  local copies, waits for them, and re-layouts: 2.85 us -> 6.04 us
  other arithmetic: 2.59 us -> 0 us
    pallas_call x0 -> x1, Pallas kernels: none -> 48.7 us  [shards(): pl.pallas_call(body, out_shape=jax.ShapeDtypeStruct((TOK, D), BF16), in_s...]
    psum x1 -> x0, waiting for transfers between devices: 43.4 us -> none  [shards(): lax.psum(linear_part.astype(jnp.bfloat16), 'dp').astype(jnp.float32)]
    all_to_all x1 -> x0, blocking collectives: 38.9 us -> none  [shards(): lax.all_to_all(token_send, 'expert', split_axis=0, concat_axis=0, tiled=T...]
    all_to_all x1 -> x0, waiting for transfers between devices: 20.4 us -> none  [shards(): lax.all_to_all(output_part.reshape(members, local_tokens, features), 'exp...]
    all_to_all x1 -> x0, starting transfers between devices: 16.6 us -> none  [shards(): lax.all_to_all(output_part.reshape(members, local_tokens, features), 'exp...]
    unnamed x10 -> x13, local copies, waits for them, and re-layouts: 0.94 us -> 6.04 us
    dot_general x4 -> x0, matrix products: 3.71 us -> none  [the longest x1 1.37 us: contract_last(): lax.dot_general(left_side, right_side, (((1,), (1,)), ((), ())), preferre...]
  transfers between devices with their start and end apart: 2 -> 0, of which waited for: 2 -> 0; matrix products, arithmetic and copies ran while one was open for 0% -> 0% of each run, Pallas kernels for 0% -> 0%
where the time goes in v1:
time: 55.1 us; the launch traced here: 54.8 us
  Pallas kernels  48.7 us (88%)
  local copies, waits for them, and re-layouts  6.04 us (11%)
    pallas_call x1, Pallas kernels, shards(): pl.pallas_call(body, out_shape=jax.ShapeDtypeStruct((TOK, D), BF16), in_s...  48.7 us
    unnamed x13, local copies, waits for them, and re-layouts  6.04 us

profile of v1, /device:TPU:1, one launch (start us, length us, event | category | flops | bytes accessed | tf_op | source)
XLA Modules:
  0.0 54.8 jit_solution(8514263505725702619)
XLA Ops:
  0.0 0.0 copy-start
  0.0 1.1 %copy-done = bf16[384,1024]{1,0:T(8,128)(2,1)S(1)} copy-done((bf16[384,1024]{1,0:T(8,128)(2,1)S(1)}, bf16[384,1024]{1,0:T(8,128)(2,1)}, u32[]{:S(2)}) %copy-start) | copy-done | bytes 786456
  1.1 0.0 copy-start.1
  1.1 1.1 %copy-done.1 = bf16[384,1024]{1,0:T(8,128)(2,1)S(1)} copy-done((bf16[384,1024]{1,0:T(8,128)(2,1)S(1)}, bf16[384,1024]{1,0:T(8,128)(2,1)}, u32[]{:S(2)}) %copy-start.1) | copy-done | bytes 786456
  2.3 0.0 copy-start.2
  2.3 1.1 %copy-done.2 = bf16[384,1024]{1,0:T(8,128)(2,1)S(1)} copy-done((bf16[384,1024]{1,0:T(8,128)(2,1)S(1)}, bf16[384,1024]{1,0:T(8,128)(2,1)}, u32[]{:S(2)}) %copy-start.2) | copy-done | bytes 786456
  3.4 0.0 copy-start.3
  3.4 0.7 %copy-done.3 = bf16[2,1024]{1,0:T(2,128)(2,1)S(1)} copy-done((bf16[2,1024]{1,0:T(2,128)(2,1)S(1)}, bf16[2,1024]{1,0:T(2,128)(2,1)}, u32[]{:S(2)}) %copy-start.3) | copy-done | bytes 4120
  4.1 0.0 copy-start.4
  4.1 0.7 %copy-done.4 = s32[2,8]{1,0:T(2,128)S(1)} copy-done((s32[2,8]{1,0:T(2,128)S(1)}, s32[2,8]{1,0:T(2,128)}, u32[]{:S(2)}) %copy-start.4) | copy-done | bytes 88
  4.8 0.0 copy-start.5
  4.8 0.7 %copy-done.5 = f32[2,8]{1,0:T(2,128)S(1)} copy-done((f32[2,8]{1,0:T(2,128)S(1)}, f32[2,8]{1,0:T(2,128)}, u32[]{:S(2)}) %copy-start.5) | copy-done | bytes 88
  5.4 48.7 %shard_map.64 = bf16[2,1024]{1,0:T(2,128)(2,1)S(1)} custom-call(bf16[2,1024]{1,0:T(2,128)(2,1)S(1)} %copy-done.3, s32[2,8]{1,0:T(2,128)S(1)} %copy-done.4, f32[2,8]{1,0:T(2,128)S(1)} %copy-done.5, bf16[384,1024]{1,0:T(8,128)(2,1)S(1)} %copy-done, bf16[384,1024]{1,0:T(8,128)(2,1)S(1)} %copy-done.1, bf16[384,1024]{1,0:T(8,128)(2,1)S(1)} %copy-done.2), custom_call_target="tpu_custom_call" | custom-call | flops 603979776 | bytes 2400000 | tf_op jit(solution)/shard_map/pallas_call | solution.py:152
  54.2 0.6 %copy.8 = bf16[2,1024]{1,0:T(2,128)(2,1)} copy(bf16[2,1024]{1,0:T(2,128)(2,1)S(1)} %shard_map.64) | data formatting | bytes 8192
Async XLA Ops:
  0.0 1.1 %copy-start = (bf16[384,1024]{1,0:T(8,128)(2,1)S(1)}, bf16[384,1024]{1,0:T(8,128)(2,1)}, u32[]{:S(2)}) copy-start(bf16[384,1024]{1,0:T(8,128)(2,1)} %gate_hbm.1) | copy-start | bytes 2359300
  1.1 1.1 %copy-start.1 = (bf16[384,1024]{1,0:T(8,128)(2,1)S(1)}, bf16[384,1024]{1,0:T(8,128)(2,1)}, u32[]{:S(2)}) copy-start(bf16[384,1024]{1,0:T(8,128)(2,1)} %up_hbm.1) | copy-start | bytes 2359300
  2.3 1.1 %copy-start.2 = (bf16[384,1024]{1,0:T(8,128)(2,1)S(1)}, bf16[384,1024]{1,0:T(8,128)(2,1)}, u32[]{:S(2)}) copy-start(bf16[384,1024]{1,0:T(8,128)(2,1)} %down_hbm.1) | copy-start | bytes 2359300
  3.4 0.7 %copy-start.3 = (bf16[2,1024]{1,0:T(2,128)(2,1)S(1)}, bf16[2,1024]{1,0:T(2,128)(2,1)}, u32[]{:S(2)}) copy-start(bf16[2,1024]{1,0:T(2,128)(2,1)} %tokens.1) | copy-start | bytes 12292
  4.1 0.7 %copy-start.4 = (s32[2,8]{1,0:T(2,128)S(1)}, s32[2,8]{1,0:T(2,128)}, u32[]{:S(2)}) copy-start(s32[2,8]{1,0:T(2,128)} %routing.1) | copy-start | bytes 196
  4.8 0.7 %copy-start.5 = (f32[2,8]{1,0:T(2,128)S(1)}, f32[2,8]{1,0:T(2,128)}, u32[]{:S(2)}) copy-start(f32[2,8]{1,0:T(2,128)} %combine.1) | copy-start | bytes 196

commit v2 on v1

--- a/solution.py
+++ b/solution.py
@@ -17,8 +17,8 @@
 EXPERTS = 32
 
 
-def body(tokens, routing, combine, gate_hbm, up_hbm, down_hbm, out,
-         gate, up, down, pay, rows1, stage, gath, part, rs, hid, own, away, other, red, rows2, tmp,
+def body(tokens_hbm, routing_hbm, combine_hbm, gate_hbm, up_hbm, down_hbm, out,
+         tokens, routing, combine, gate, up, down, pay, rows1, stage, gath, part, rs, hid, own, away, other, red, rows2, tmp,
          wsem, s1, r1, s2, r2, s3, r3, s4, r4, s5, r5, s6, r6, s7, r7, s8, r8):
     me = lax.axis_index("expert")
     x = lax.axis_index("dp")
@@ -51,10 +51,13 @@
         pl.semaphore_signal(barrier, inc=1, device_id=over(d), device_id_type=MESH)
     pl.semaphore_signal(barrier, inc=1, device_id=partner, device_id_type=MESH)
 
-    loads = [pltpu.make_async_copy(src, dst, wsem.at[i])
-             for i, (src, dst) in enumerate(((gate_hbm, gate), (up_hbm, up), (down_hbm, down)))]
+    loads = [pltpu.make_async_copy(src, dst, wsem.at[i]) for i, (src, dst) in enumerate((
+        (tokens_hbm, tokens), (routing_hbm, routing), (combine_hbm, combine),
+        (gate_hbm, gate), (up_hbm, up), (down_hbm, down)))]
     for cp in loads:
         cp.start()
+    for cp in loads[:3]:
+        cp.wait()
 
     pay[:, :D] = tokens[...]
     lane = lax.broadcasted_iota(jnp.int32, (TOK, 128), 1)
@@ -77,7 +80,7 @@
     for d in NEAR:
         c2[d].wait_recv()
         c3[d] = send(gath.at[0, d], gath.at[1, d], s3.at[d], r3.at[d], partner)
-    for cp in loads:
+    for cp in loads[3:]:
         cp.wait()
 
     def linear(h):
@@ -152,9 +155,10 @@
     return pl.pallas_call(
         body,
         out_shape=jax.ShapeDtypeStruct((TOK, D), BF16),
-        in_specs=[vmem, vmem, vmem, hbm, hbm, hbm],
+        in_specs=[hbm] * 6,
         out_specs=vmem,
         scratch_shapes=[
+            pltpu.VMEM((TOK, D), BF16), pltpu.VMEM((TOK, 8), jnp.int32), pltpu.VMEM((TOK, 8), F32),
             pltpu.VMEM((H, D), BF16), pltpu.VMEM((H, D), BF16), pltpu.VMEM((H, D), BF16),
             pltpu.VMEM((TOK, PAY), BF16),
             pltpu.VMEM((LINE, TOK, PAY), BF16),
@@ -169,13 +173,13 @@
             pltpu.VMEM((LINE, BLK, D), BF16),
             pltpu.VMEM((2, LINE, TOK, D), BF16),
             pltpu.VMEM((LINE, BLK, D), BF16),
-            dma((3,)),
+            dma((6,)),
             dma((8,)), dma((8,)), dma((8,)), dma((8,)), dma((8,)), dma((8,)),
             dma((2, 4)), dma((2, 4)), dma((2, 4)), dma((2, 4)),
             dma((8,)), dma((8,)), dma((8,)), dma((8,)), dma((8,)), dma((8,)),
         ],
         compiler_params=pltpu.CompilerParams(
-            collective_id=0, has_side_effects=True, vmem_limit_bytes=48 << 20),
+            collective_id=0, has_side_effects=True, vmem_limit_bytes=60 << 20),
         cost_estimate=pl.CostEstimate(flops=603979776, bytes_accessed=2400000, transcendentals=24576),
     )(tokens, routing, combine, gate, up, down)
 

time: 55.1 us -> 50.8 us (0.922)
  local copies, waits for them, and re-layouts: 6.04 us -> 1.28 us
  Pallas kernels: 48.7 us -> 49.4 us
    unnamed x13 -> x1, local copies, waits for them, and re-layouts: 6.04 us -> 1.28 us
    pallas_call x1, Pallas kernels: 48.7 us -> 49.4 us  [shards(): pl.pallas_call(body, out_shape=jax.ShapeDtypeStruct((TOK, D), BF16), in_s...]
where the time goes in v2:
time: 50.8 us; the launch traced here: 50.6 us
  Pallas kernels  49.4 us (97%)
  local copies, waits for them, and re-layouts  1.28 us (3%)
    pallas_call x1, Pallas kernels, shards(): pl.pallas_call(body, out_shape=jax.ShapeDtypeStruct((TOK, D), BF16), in_s...  49.4 us
    unnamed x1, local copies, waits for them, and re-layouts  1.28 us

profile of v2, /device:TPU:1, one launch (start us, length us, event | category | flops | bytes accessed | tf_op | source)
XLA Modules:
  0.0 50.6 jit_solution(3024545482611660942)
XLA Ops:
  0.0 49.4 %shard_map.64 = bf16[2,1024]{1,0:T(2,128)(2,1)} custom-call(bf16[2,1024]{1,0:T(2,128)(2,1)} %tokens_hbm.1, s32[2,8]{1,0:T(2,128)} %routing_hbm.1, f32[2,8]{1,0:T(2,128)} %combine_hbm.1, bf16[384,1024]{1,0:T(8,128)(2,1)} %gate_hbm.1, bf16[384,1024]{1,0:T(8,128)(2,1)} %up_hbm.1, bf16[384,1024]{1,0:T(8,128)(2,1)} %down_hbm.1), custom_call_target="tpu_custom_call" | custom-call | flops 603979776 | bytes 2400000 | tf_op jit(solution)/shard_map/pallas_call | solution.py:155
  49.4 1.3 %copy.8 = bf16[2,1024]{1,0:T(2,128)(2,1)} copy(bf16[2,1024]{1,0:T(2,128)(2,1)} %shard_map.64) | data formatting | bytes 8192

commit v3 on v2

v3 whole, which is shorter than its diff:
```python
import jax
import jax.numpy as jnp
from jax import lax
from jax.experimental import pallas as pl
from jax.experimental.pallas import tpu as pltpu
from jax.sharding import PartitionSpec as P

MESH = pl.DeviceIdType.MESH
F32, BF16 = jnp.float32, jnp.bfloat16
LINE = 8
FAR = (4, 3, 5, 2, 6, 1, 7)
NEAR = (1, 7, 2, 6, 3, 5, 4)
DP = (2, 1, 3)
D, H, PAY = 1024, 384, 1152
TOK, BLK, HALF = 2, 16, 8
SLICES = 4
EXPERTS = 32


def body(tokens_hbm, routing_hbm, combine_hbm, gate_hbm, up_hbm, down_hbm, out,
         tokens, routing, combine, gate, up, down, pay, rows1, stage, gath, part, rs, hid, perm,
         own, away, other, tmp, red, zf, zsend, zrecv,
         wsem, insem, s1, r1, s2, r2, s3, r3, s4, r4, s5, r5, s6, r6, s7, r7, s8, r8):
    me = lax.axis_index("expert")
    x = lax.axis_index("dp")
    c = lax.rem(me, 2)
    y = lax.rem(me // 2, LINE)
    z = me // (2 * LINE)
    e = me // SLICES
    partner = (me + 1 - 2 * c, x)

    def along_y(d):
        return ((z * LINE + lax.rem(y + d, LINE)) * 2 + c, x)

    def at_z(zz):
        return ((zz * LINE + y) * 2 + c, x)

    def over(d):
        return (me, lax.rem(x + d, 4))

    def copy(src, dst, ssem, rsem, to):
        return pltpu.make_async_remote_copy(
            src_ref=src, dst_ref=dst, send_sem=ssem, recv_sem=rsem, device_id=to, device_id_type=MESH)

    def send(*args):
        cp = copy(*args)
        cp.start()
        return cp

    def signal(sem, to):
        pl.semaphore_signal(sem, inc=1, device_id=to, device_id_type=MESH)

    barrier = pltpu.get_barrier_semaphore()
    for d in FAR:
        signal(barrier, along_y(d))
    for d in DP:
        signal(barrier, over(d))
    signal(barrier, partner)
    for zs in range(1, LINE):
        @pl.when(zs > z)
        def _():
            signal(barrier, at_z(zs))

    loads = [pltpu.make_async_copy(src, dst, wsem.at[i]) for i, (src, dst) in enumerate((
        (tokens_hbm, tokens), (routing_hbm, routing), (combine_hbm, combine),
        (gate_hbm, gate), (up_hbm, up), (down_hbm, down)))]
    for cp in loads:
        cp.start()
    for cp in loads[:3]:
        cp.wait()

    pay[:, :D] = tokens[...]
    lane = lax.broadcasted_iota(jnp.int32, (TOK, 128), 1)
    dense = jnp.zeros((TOK, 128), F32)
    for k in range(8):
        dense = dense + jnp.where(lax.rem(lane, EXPERTS) == routing[:, k:k + 1], combine[:, k:k + 1], 0.0)
    high = dense.astype(BF16).astype(F32)
    pay[:, D:] = jnp.where(lane < EXPERTS, high, jnp.where(lane < 2 * EXPERTS, dense - high, 0.0)).astype(BF16)
    pl.semaphore_wait(barrier, 11 + z)
    for zs in range(LINE - 1):
        @pl.when(zs < z)
        def _():
            signal(insem.at[z], at_z(zs))

    c1 = {d: send(pay, rows1.at[d], s1.at[d], r1.at[d], along_y(d)) for d in FAR}
    stage[0:TOK, :] = pay[...].astype(F32)

    r = lax.broadcasted_iota(jnp.int32, (128, 128), 0)
    k = lax.broadcasted_iota(jnp.int32, (128, 128), 1)
    core = lax.rem(r // 64 + c, 2)
    source = lax.rem(r // 2, 4) * 32 + core * 16 + lax.rem(r // 8, 8) * 2 + lax.rem(r, 2)
    perm[...] = jnp.where(k == source, 1.0, 0.0).astype(BF16)

    for d in NEAR:
        c1[d].wait_recv()
        stage[TOK * d:TOK * d + TOK, :] = rows1[d].astype(F32)
    gath[z, c] = stage[...].astype(BF16)

    mine = gath.at[z, c]
    send(mine, mine, s3.at[z], r3.at[z], partner)
    for zs in range(LINE):
        @pl.when(zs > z)
        def _():
            pl.semaphore_wait(insem.at[zs], 1)

        @pl.when(zs != z)
        def _():
            send(mine, mine, s2.at[zs], r2.at[z], at_z(zs))

    def block(zs):
        return copy(gath.at[zs, c], gath.at[zs, c], s2.at[zs], r2.at[zs], partner)

    def onward(zs):
        return copy(gath.at[zs, c], gath.at[zs, c], s3.at[zs], r3.at[zs], partner)

    def take(g):
        for zs in range(4 * g, 4 * g + 4):
            @pl.when(zs != z)
            def _():
                block(zs).wait_recv()
                onward(zs).start()

    def meet(g):
        for zs in range(4 * g, 4 * g + 4):
            copy(gath.at[zs, 1 - c], gath.at[zs, 1 - c], s3.at[zs], r3.at[zs], partner).wait_recv()

    def linear(g):
        rows = gath[4 * g:4 * g + 4, :, :, :D].reshape(128, D)
        for i, w in enumerate((gate, up)):
            lin = lax.dot_general(rows, w[...], (((1,), (1,)), ((), ())), preferred_element_type=F32)
            part[g, :, :, i * H:(i + 1) * H] = lin.astype(BF16).reshape(4, 32, H)
        return {d: send(part.at[g, lax.rem(x + d, 4)], rs.at[g, d], s4.at[g, d], r4.at[g, d], over(d)) for d in DP}

    lanes = lax.broadcasted_iota(jnp.int32, (32, 128), 1)
    named = (lanes == e) | (lanes == e + EXPERTS)

    def activate(g, c4):
        total = part[g, x].astype(F32)
        for d in (1, 3, 2):
            c4[d].wait_recv()
            total = total + rs[g, d].astype(F32)
        wrow = gath[4 * g + x, :, :, D:].reshape(32, 128).astype(F32)
        weight = jnp.sum(jnp.where(named, wrow, 0.0), axis=1, keepdims=True)
        gt, u = total[:, :H], total[:, H:]
        hid[g, x] = (jax.nn.sigmoid(gt) * gt * u * weight).astype(BF16)
        return {d: send(hid.at[g, x], hid.at[g, x], s5.at[g, d], r5.at[g, d], over(d)) for d in DP}

    def arrived(g):
        for d in (1, 3, 2):
            src = lax.rem(x + 4 - d, 4)
            copy(hid.at[g, src], hid.at[g, src], s5.at[g, d], r5.at[g, d], over(d)).wait_recv()

    def product(g):
        arrived(g)
        h = jnp.dot(perm[...], hid[g].reshape(128, H), preferred_element_type=F32).astype(BF16)
        away[g] = jnp.dot(h[64:], down[...], preferred_element_type=F32).astype(BF16).reshape(LINE, HALF, D)
        cp = send(away.at[g], other.at[g], s6.at[g], r6.at[g], partner)
        own[g] = jnp.dot(h[:64], down[...], preferred_element_type=F32).reshape(LINE, HALF, D)
        return cp

    def cores(g, c6):
        c6.wait_recv()
        c7 = {}
        for d in FAR:
            tmp[g, d] = (own[g, d] + other[g, d].astype(F32)).astype(BF16)
            c7[d] = send(tmp.at[g, d], red.at[g, d], s7.at[g, d], r7.at[g, d], along_y(LINE - d))
        own[g, 0] = own[g, 0] + other[g, 0].astype(F32)
        return c7

    def line(g, c7):
        total = own[g, 0]
        for d in NEAR:
            c7[d].wait_recv()
            total = total + red[g, d].astype(F32)
        own[g, 0] = total
        for q in range(4):
            piece = own[g, 0, TOK * q:TOK * q + TOK, :]
            zf[4 * g + q] = piece
            zsend[4 * g + q] = piece.astype(BF16)

            @pl.when(4 * g + q != z)
            def _():
                send(zsend.at[4 * g + q], zrecv.at[z], s8.at[4 * g + q], r8.at[z], at_z(4 * g + q))

    take(0)
    for cp in loads[3:]:
        cp.wait()
    meet(0)
    c40 = linear(0)
    take(1)
    c50 = activate(0, c40)
    meet(1)
    c41 = linear(1)
    c60 = product(0)
    c51 = activate(1, c41)
    c70 = cores(0, c60)
    c61 = product(1)
    line(0, c70)
    c71 = cores(1, c61)
    line(1, c71)

    final = zf[z]
    for d in NEAR:
        src = lax.rem(z + d, LINE)
        copy(zsend.at[src], zrecv.at[src], s8.at[src], r8.at[src], partner).wait_recv()
        final = final + zrecv[src].astype(F32)
    out[...] = final.astype(BF16)

    for group in (c1, c40, c41, c50, c51, c70, c71):
        for cp in group.values():
            cp.wait_send()
    c60.wait_send()
    c61.wait_send()
    for zs in range(LINE):
        onward(zs).wait_send()

        @pl.when(zs != z)
        def _():
            block(zs).wait_send()
            copy(zsend.at[zs], zrecv.at[zs], s8.at[zs], r8.at[zs], partner).wait_send()


def shards(tokens, routing, combine, gate, up, down):
    hbm = pl.BlockSpec(memory_space=pl.ANY)
    dma = pltpu.SemaphoreType.DMA
    return pl.pallas_call(
        body,
        out_shape=jax.ShapeDtypeStruct((TOK, D), BF16),
        in_specs=[hbm] * 6,
        out_specs=pl.BlockSpec(memory_space=pltpu.VMEM),
        scratch_shapes=[
            pltpu.VMEM((TOK, D), BF16), pltpu.VMEM((TOK, 8), jnp.int32), pltpu.VMEM((TOK, 8), F32),
            pltpu.VMEM((H, D), BF16), pltpu.VMEM((H, D), BF16), pltpu.VMEM((H, D), BF16),
            pltpu.VMEM((TOK, PAY), BF16),
            pltpu.VMEM((LINE, TOK, PAY), BF16),
            pltpu.VMEM((BLK, PAY), F32),
            pltpu.VMEM((LINE, 2, BLK, PAY), BF16),
            pltpu.VMEM((2, 4, 32, 2 * H), BF16),
            pltpu.VMEM((2, 4, 32, 2 * H), BF16),
            pltpu.VMEM((2, 4, 32, H), BF16),
            pltpu.VMEM((128, 128), BF16),
            pltpu.VMEM((2, LINE, HALF, D), F32),
            pltpu.VMEM((2, LINE, HALF, D), BF16),
            pltpu.VMEM((2, LINE, HALF, D), BF16),
            pltpu.VMEM((2, LINE, HALF, D), BF16),
            pltpu.VMEM((2, LINE, HALF, D), BF16),
            pltpu.VMEM((LINE, TOK, D), F32),
            pltpu.VMEM((LINE, TOK, D), BF16),
            pltpu.VMEM((LINE, TOK, D), BF16),
            dma((6,)), pltpu.SemaphoreType.REGULAR((8,)),
            dma((8,)), dma((8,)), dma((8,)), dma((8,)), dma((8,)), dma((8,)),
            dma((2, 4)), dma((2, 4)), dma((2, 4)), dma((2, 4)),
            dma((2,)), dma((2,)), dma((2, 8)), dma((2, 8)), dma((8,)), dma((8,)),
        ],
        compiler_params=pltpu.CompilerParams(
            collective_id=0, has_side_effects=True, vmem_limit_bytes=60 << 20),
        cost_estimate=pl.CostEstimate(flops=603979776, bytes_accessed=2400000, transcendentals=24576),
    )(tokens, routing, combine, gate, up, down)


def solution(mesh):
    return jax.shard_map(
        shards,
        mesh=mesh,
        in_specs=(
            P("expert", "dp"),
            P("expert", None),
            P("expert", None),
            P("expert", "dp"),
            P("expert", "dp"),
            P("expert", "dp"),
        ),
        out_specs=P("expert", "dp"),
        check_vma=False,
    )
```

time: 50.8 us -> 48.1 us (0.947)
  Pallas kernels: 49.4 us -> 46.7 us
    pallas_call x1, Pallas kernels: 49.4 us -> 46.7 us  [shards(): pl.pallas_call(body, out_shape=jax.ShapeDtypeStruct((TOK, D), BF16), in_s...]
where the time goes in v3:
time: 48.1 us; the launch traced here: 47.9 us
  Pallas kernels  46.7 us (97%)
  local copies, waits for them, and re-layouts  1.28 us (3%)
    pallas_call x1, Pallas kernels, shards(): pl.pallas_call(body, out_shape=jax.ShapeDtypeStruct((TOK, D), BF16), in_s...  46.7 us
    unnamed x1, local copies, waits for them, and re-layouts  1.28 us

profile of v3, /device:TPU:1, one launch (start us, length us, event | category | flops | bytes accessed | tf_op | source)
XLA Modules:
  0.0 47.9 jit_solution(5396627178566877828)
XLA Ops:
  0.0 46.7 %shard_map.64 = bf16[2,1024]{1,0:T(2,128)(2,1)} custom-call(bf16[2,1024]{1,0:T(2,128)(2,1)} %tokens_hbm.1, s32[2,8]{1,0:T(2,128)} %routing_hbm.1, f32[2,8]{1,0:T(2,128)} %combine_hbm.1, bf16[384,1024]{1,0:T(8,128)(2,1)} %gate_hbm.1, bf16[384,1024]{1,0:T(8,128)(2,1)} %up_hbm.1, bf16[384,1024]{1,0:T(8,128)(2,1)} %down_hbm.1), custom_call_target="tpu_custom_call" | custom-call | flops 603979776 | bytes 2400000 | tf_op jit(solution)/shard_map/pallas_call | solution.py:226
  46.7 1.3 %copy.8 = bf16[2,1024]{1,0:T(2,128)(2,1)} copy(bf16[2,1024]{1,0:T(2,128)(2,1)} %shard_map.64) | data formatting | bytes 8192

commit v4 on v3

v4 whole, which is shorter than its diff:
```python
import jax
import jax.numpy as jnp
from jax import lax
from jax.experimental import pallas as pl
from jax.experimental.pallas import tpu as pltpu
from jax.sharding import PartitionSpec as P

MESH = pl.DeviceIdType.MESH
F32, BF16 = jnp.float32, jnp.bfloat16
LINE = 8
FAR = (4, 3, 5, 2, 6, 1, 7)
NEAR = (1, 7, 2, 6, 3, 5, 4)
EARLY = (0, 1, 2, 3, 7, 6, 5, 4)
D, H, PAY = 1024, 384, 1152
TOK, BLK = 2, 16
GROUPS = 4
DEEP = LINE // GROUPS
ROWS = DEEP * 2 * BLK
PART = ROWS // 4
PIECE = DEEP * TOK
EARLIER = 3
MID = EARLIER * DEEP
SLICES = 4
EXPERTS = 32


def body(tokens_hbm, routing_hbm, combine_hbm, gate_hbm, up_hbm, down_hbm, out,
         tokens, routing, combine, gate, up, turned, down, pay, rows1, stage, gath, part, rs, hid, perm,
         perm2, own, away, other, tmp, red, zf, zsend, zrecv,
         own2, away2, other2, tmp2, red2, sum2, ysend, yrecv,
         wsem, inz, iny, inx, inc, s1, r1, s2, r2, s3, r3, s4, r4, s5, r5, s6, r6, s7, r7, s8, r8, s9, r9, s10, r10):
    me = lax.axis_index("expert")
    x = lax.axis_index("dp")
    c = lax.rem(me, 2)
    y = lax.rem(me // 2, LINE)
    z = me // (2 * LINE)
    e = me // SLICES
    partner = (me + 1 - 2 * c, x)

    def at_y(yy):
        return ((z * LINE + yy) * 2 + c, x)

    def along_y(d):
        return at_y(lax.rem(y + d, LINE))

    def at_z(zz):
        return ((zz * LINE + y) * 2 + c, x)

    def copy(src, dst, ssem, rsem, to):
        return pltpu.make_async_remote_copy(
            src_ref=src, dst_ref=dst, send_sem=ssem, recv_sem=rsem, device_id=to, device_id_type=MESH)

    def send(*args):
        cp = copy(*args)
        cp.start()
        return cp

    def signal(sem, to):
        pl.semaphore_signal(sem, inc=1, device_id=to, device_id_type=MESH)

    barrier = pltpu.get_barrier_semaphore()
    rank = y + (y // 4) * (11 - 2 * y)

    def later(act):
        for zs in range(1, LINE):
            @pl.when(zs > z)
            def _():
                act(at_z(zs))
        for i, ys in enumerate(EARLY):
            @pl.when(i > rank)
            def _():
                act(at_y(ys))
        for xs in range(1, 4):
            @pl.when(xs > x)
            def _():
                act((me, xs))

        @pl.when(c == 1)
        def _():
            act(partner)

    later(lambda to: signal(barrier, to))
    loads = [pltpu.make_async_copy(src, dst, wsem.at[i]) for i, (src, dst) in enumerate((
        (tokens_hbm, tokens), (routing_hbm, routing), (combine_hbm, combine),
        (gate_hbm, gate), (up_hbm, up), (down_hbm, down)))]
    for cp in loads:
        cp.start()
    for cp in loads[:3]:
        cp.wait()
    pay[:, :D] = tokens[...]
    lane = lax.broadcasted_iota(jnp.int32, (TOK, 128), 1)
    number = jnp.where(lane < EXPERTS, lane, lane - EXPERTS)
    dense = jnp.zeros((TOK, 128), F32)
    for k in range(8):
        dense = dense + jnp.where(number == routing[:, k:k + 1], combine[:, k:k + 1], 0.0)
    high = dense.astype(BF16).astype(F32)
    pay[:, D:] = jnp.where(lane < EXPERTS, high, jnp.where(lane < 2 * EXPERTS, dense - high, 0.0)).astype(BF16)

    before = z + rank + x + 1 - c

    @pl.when(before > 0)
    def _():
        pl.semaphore_wait(barrier, before)

    for zs in range(LINE - 1):
        @pl.when(zs < z)
        def _():
            signal(inz.at[z], at_z(zs))
    for i, ys in enumerate(EARLY):
        @pl.when(i < rank)
        def _():
            signal(iny.at[y], at_y(ys))
    for xs in range(3):
        @pl.when(xs < x)
        def _():
            signal(inx.at[x], (me, xs))

    @pl.when(c == 0)
    def _():
        signal(inc, partner)

    for i, ys in enumerate(EARLY):
        @pl.when(i > rank)
        def _():
            pl.semaphore_wait(iny.at[ys], 1)

        @pl.when(i != rank)
        def _():
            d = lax.rem(ys - y + LINE, LINE)
            send(pay, rows1.at[d], s1.at[d], r1.at[d], at_y(ys))
    stage[0:TOK, :] = pay[...].astype(F32)

    def greeting(d):
        return copy(pay, rows1.at[d], s1.at[d], r1.at[d], partner)

    r = lax.broadcasted_iota(jnp.int32, (ROWS, ROWS), 0)
    k = lax.broadcasted_iota(jnp.int32, (ROWS, ROWS), 1)
    core = (r // (ROWS // 2) + c) & 1
    place = (r // PIECE) & 7
    dist = 4 + ((place + 1) // 2) * (1 - 2 * (place & 1))
    source = ((r // 2) & (DEEP - 1)) * 32 + core * 16 + dist * 2 + (r & 1)
    perm[...] = jnp.where(k == source, 1.0, 0.0).astype(BF16)
    source = ((r // BLK) & (DEEP - 1)) * 32 + core * 16 + (r & 15)
    perm2[...] = jnp.where(k == source, 1.0, 0.0).astype(BF16)

    for cp in loads[3:]:
        cp.wait()
    turned[:, :H] = gate[...].T
    turned[:, H:] = up[...].T
    for d in NEAR:
        greeting(d).wait_recv()
        stage[TOK * d:TOK * d + TOK, :] = rows1[d].astype(F32)
    gath[z, c] = stage[...].astype(BF16)

    mine = gath.at[z, c]

    @pl.when(c == 1)
    def _():
        pl.semaphore_wait(inc, 1)

    send(mine, mine, s3.at[z], r3.at[z], partner)
    for zs in range(LINE):
        @pl.when(zs > z)
        def _():
            pl.semaphore_wait(inz.at[zs], 1)

        @pl.when(zs != z)
        def _():
            send(mine, mine, s2.at[zs], r2.at[z], at_z(zs))

    def block(zs):
        return copy(gath.at[zs, c], gath.at[zs, c], s2.at[zs], r2.at[zs], partner)

    def onward(zs):
        return copy(gath.at[zs, c], gath.at[zs, c], s3.at[zs], r3.at[zs], partner)

    def take(g):
        for zs in range(DEEP * g, DEEP * g + DEEP):
            @pl.when(zs != z)
            def _():
                block(zs).wait_recv()
                onward(zs).start()

    def meet(zs):
        copy(gath.at[zs, 1 - c], gath.at[zs, 1 - c], s3.at[zs], r3.at[zs], partner).wait_recv()

    def share(g, xs):
        return copy(part.at[g, xs], rs.at[g, x], s4.at[g, xs], r4.at[g, x], (me, xs))

    def linear(g):
        for zs in range(DEEP * g, DEEP * g + DEEP):
            meet(zs)
        rows = gath[DEEP * g:DEEP * g + DEEP, :, :, :D].reshape(ROWS, D)
        lin = jnp.dot(rows, turned[...], preferred_element_type=F32)
        part[g] = lin.astype(BF16).reshape(4, PART, 2 * H)
        for xs in range(4):
            if g == 0:
                @pl.when(xs > x)
                def _():
                    pl.semaphore_wait(inx.at[xs], 1)

            @pl.when(xs != x)
            def _():
                share(g, xs).start()

    lanes = lax.broadcasted_iota(jnp.int32, (PART, 128), 1)
    named = (lanes == e) | (lanes == e + EXPERTS)

    def spread(g, d):
        to = (me, lax.rem(x + d, 4))
        return copy(hid.at[g, x], hid.at[g, x], s5.at[g, d], r5.at[g, d], to)

    def activate(g):
        total = part[g, x].astype(F32)
        for d in (1, 3, 2):
            xs = lax.rem(x + d, 4)
            copy(part.at[g, xs], rs.at[g, xs], s4.at[g, xs], r4.at[g, xs], (me, xs)).wait_recv()
            total = total + rs[g, xs].astype(F32)
        wrow = gath[DEEP * g + x // 2, lax.rem(x, 2), :, D:].astype(F32)
        weight = jnp.sum(jnp.where(named, wrow, 0.0), axis=1, keepdims=True)
        gt, u = total[:, :H], total[:, H:]
        hid[g, x] = (jax.nn.sigmoid(gt) * gt * u * weight).astype(BF16)
        for d in (2, 1, 3):
            spread(g, d).start()

    def product(g):
        for d in (1, 3, 2):
            src = lax.rem(x + 4 - d, 4)
            copy(hid.at[g, src], hid.at[g, src], s5.at[g, d], r5.at[g, d], partner).wait_recv()
        early, i = g < EARLIER, g % EARLIER
        order, mine_ref, to, at, shape = (
            (perm, own, away, other, (LINE, PIECE, D)) if early else (perm2, own2, away2, other2, (DEEP, BLK, D)))
        h = jnp.dot(order[...], hid[g].reshape(ROWS, H), preferred_element_type=F32).astype(BF16)
        both = jnp.dot(h, down[...], preferred_element_type=F32)
        to[i] = both[ROWS // 2:].astype(BF16).reshape(shape)
        cp = send(to.at[i], at.at[i], s6.at[g], r6.at[g], partner)
        mine_ref[i] = both[:ROWS // 2].reshape(shape)
        return cp

    def back(zs):
        i, q = (zs - MID) // DEEP, (zs - MID) % DEEP
        return copy(tmp2.at[i, q], red2.at[z], s9.at[zs], r9.at[z], at_z(zs))

    def cores2(g, c6):
        i = g - EARLIER
        c6.wait_recv()
        for q in range(DEEP):
            zs = DEEP * g + q
            both = own2[i, q] + other2[i, q].astype(F32)
            tmp2[i, q] = both.astype(BF16)

            @pl.when(zs != z)
            def _():
                back(zs).start()

            @pl.when(zs == z)
            def _():
                sum2[...] = both

    def cores(g, c6):
        c6.wait_recv()
        c7 = {}
        for i, d in enumerate(FAR + (0,)):
            both = own[g, i] + other[g, i].astype(F32)
            if d:
                tmp[g, i] = both.astype(BF16)
                c7[d] = send(tmp.at[g, i], red.at[g, d], s7.at[g, d], r7.at[g, d], along_y(LINE - d))
            else:
                own[g, 0] = both
        return c7

    def line(g, c7):
        total = own[g, 0]
        for d in NEAR:
            c7[d].wait_recv()
            total = total + red[g, d].astype(F32)
        own[g, 0] = total
        for q in range(DEEP):
            piece = own[g, 0, TOK * q:TOK * q + TOK, :]
            zf[DEEP * g + q] = piece
            zsend[DEEP * g + q] = piece.astype(BF16)

            @pl.when(DEEP * g + q != z)
            def _():
                send(zsend.at[DEEP * g + q], zrecv.at[z], s8.at[DEEP * g + q], r8.at[z], at_z(DEEP * g + q))

    c6, c7 = {}, {}
    take(0)
    linear(0)
    take(1)
    linear(1)
    activate(0)
    take(2)
    take(3)
    linear(2)
    c6[0] = product(0)
    activate(1)
    linear(3)
    c7[0] = cores(0, c6[0])
    activate(2)
    c6[1] = product(1)
    activate(3)
    c7[1] = cores(1, c6[1])
    c6[2] = product(2)
    line(0, c7[0])
    c7[2] = cores(2, c6[2])
    c6[3] = product(3)
    cores2(3, c6[3])
    line(1, c7[1])
    line(2, c7[2])

    @pl.when(z < MID)
    def _():
        final = zf[z]
        for d in NEAR:
            src = lax.rem(z + d, LINE)
            copy(zsend.at[0], zrecv.at[src], s8.at[0], r8.at[src], partner).wait_recv()
            final = final + zrecv[src].astype(F32)
        out[...] = final.astype(BF16)

    def row(d):
        return copy(ysend.at[d], yrecv.at[d], s10.at[d], r10.at[d], along_y(LINE - d))

    @pl.when(z >= MID)
    def _():
        total = sum2[...]
        for d in NEAR:
            src = lax.rem(z + d, LINE)
            copy(tmp2.at[0, 0], red2.at[src], s9.at[src], r9.at[src], partner).wait_recv()
            total = total + red2[src].astype(F32)
        sum2[...] = total
        for d in FAR:
            ysend[d] = sum2[TOK * d:TOK * d + TOK, :].astype(BF16)
            row(d).start()
        final = sum2[0:TOK, :]
        for d in NEAR:
            row(d).wait_recv()
            final = final + yrecv[d].astype(F32)
        out[...] = final.astype(BF16)
        for d in NEAR:
            row(d).wait_send()

    for g in range(GROUPS):
        c6[g].wait_send()
        for cp in c7[g].values() if g in c7 else ():
            cp.wait_send()
        for d in (1, 2, 3):
            spread(g, d).wait_send()
        for xs in range(4):
            @pl.when(xs != x)
            def _():
                share(g, xs).wait_send()
    for d in NEAR:
        greeting(d).wait_send()
    for zs in range(LINE):
        onward(zs).wait_send()

        @pl.when(zs != z)
        def _():
            block(zs).wait_send()
            if zs < MID:
                copy(zsend.at[zs], zrecv.at[z], s8.at[zs], r8.at[z], partner).wait_send()
            else:
                back(zs).wait_send()


def shards(tokens, routing, combine, gate, up, down):
    hbm = pl.BlockSpec(memory_space=pl.ANY)
    dma, flag = pltpu.SemaphoreType.DMA, pltpu.SemaphoreType.REGULAR
    return pl.pallas_call(
        body,
        out_shape=jax.ShapeDtypeStruct((TOK, D), BF16),
        in_specs=[hbm] * 6,
        out_specs=pl.BlockSpec(memory_space=pltpu.VMEM),
        scratch_shapes=[
            pltpu.VMEM((TOK, D), BF16), pltpu.VMEM((TOK, 8), jnp.int32), pltpu.VMEM((TOK, 8), F32),
            pltpu.VMEM((H, D), BF16), pltpu.VMEM((H, D), BF16), pltpu.VMEM((D, 2 * H), BF16), pltpu.VMEM((H, D), BF16),
            pltpu.VMEM((TOK, PAY), BF16),
            pltpu.VMEM((LINE, TOK, PAY), BF16),
            pltpu.VMEM((BLK, PAY), F32),
            pltpu.VMEM((LINE, 2, BLK, PAY), BF16),
            pltpu.VMEM((GROUPS, 4, PART, 2 * H), BF16),
            pltpu.VMEM((GROUPS, 4, PART, 2 * H), BF16),
            pltpu.VMEM((GROUPS, 4, PART, H), BF16),
            pltpu.VMEM((ROWS, ROWS), BF16), pltpu.VMEM((ROWS, ROWS), BF16),
            pltpu.VMEM((EARLIER, LINE, PIECE, D), F32),
            pltpu.VMEM((EARLIER, LINE, PIECE, D), BF16),
            pltpu.VMEM((EARLIER, LINE, PIECE, D), BF16),
            pltpu.VMEM((EARLIER, LINE, PIECE, D), BF16),
            pltpu.VMEM((EARLIER, LINE, PIECE, D), BF16),
            pltpu.VMEM((MID, TOK, D), F32),
            pltpu.VMEM((MID, TOK, D), BF16),
            pltpu.VMEM((LINE, TOK, D), BF16),
            pltpu.VMEM((EARLIER, DEEP, BLK, D), F32),
            pltpu.VMEM((EARLIER, DEEP, BLK, D), BF16),
            pltpu.VMEM((EARLIER, DEEP, BLK, D), BF16),
            pltpu.VMEM((EARLIER, DEEP, BLK, D), BF16),
            pltpu.VMEM((LINE, BLK, D), BF16),
            pltpu.VMEM((BLK, D), F32),
            pltpu.VMEM((LINE, TOK, D), BF16),
            pltpu.VMEM((LINE, TOK, D), BF16),
            dma((6,)), flag((8,)), flag((8,)), flag((4,)), flag,
            dma((8,)), dma((8,)), dma((8,)), dma((8,)), dma((8,)), dma((8,)),
            dma((GROUPS, 4)), dma((GROUPS, 4)), dma((GROUPS, 4)), dma((GROUPS, 4)),
            dma((GROUPS,)), dma((GROUPS,)), dma((GROUPS, 8)), dma((GROUPS, 8)), dma((8,)), dma((8,)),
            dma((8,)), dma((8,)), dma((8,)), dma((8,)),
        ],
        compiler_params=pltpu.CompilerParams(
            collective_id=0, has_side_effects=True, vmem_limit_bytes=60 << 20),
        cost_estimate=pl.CostEstimate(flops=603979776, bytes_accessed=2400000, transcendentals=24576),
    )(tokens, routing, combine, gate, up, down)


def solution(mesh):
    return jax.shard_map(
        shards,
        mesh=mesh,
        in_specs=(
            P("expert", "dp"),
            P("expert", None),
            P("expert", None),
            P("expert", "dp"),
            P("expert", "dp"),
            P("expert", "dp"),
        ),
        out_specs=P("expert", "dp"),
        check_vma=False,
    )
```

time: 48.1 us -> 47.6 us (0.990)
  the two profiles are of different devices: /device:TPU:1 before, /device:TPU:448 now
where the time goes in v4:
time: 47.6 us; the launch traced here: 47.5 us
  Pallas kernels  46.2 us (97%)
  local copies, waits for them, and re-layouts  1.28 us (3%)
    pallas_call x1, Pallas kernels, shards(): pl.pallas_call(body, out_shape=jax.ShapeDtypeStruct((TOK, D), BF16), in_s...  46.2 us
    unnamed x1, local copies, waits for them, and re-layouts  1.28 us

profile of v4, /device:TPU:448, one launch (start us, length us, event | category | flops | bytes accessed | tf_op | source)
XLA Modules:
  0.0 47.5 jit_solution(9265697286298975141)
XLA Ops:
  0.0 46.2 %shard_map.64 = bf16[2,1024]{1,0:T(2,128)(2,1)} custom-call(bf16[2,1024]{1,0:T(2,128)(2,1)} %tokens_hbm.1, s32[2,8]{1,0:T(2,128)} %routing_hbm.1, f32[2,8]{1,0:T(2,128)} %combine_hbm.1, bf16[384,1024]{1,0:T(8,128)(2,1)} %gate_hbm.1, bf16[384,1024]{1,0:T(8,128)(2,1)} %up_hbm.1, bf16[384,1024]{1,0:T(8,128)(2,1)} %down_hbm.1), custom_call_target="tpu_custom_call" | custom-call | flops 603979776 | bytes 2400000 | tf_op jit(solution)/shard_map/pallas_call | solution.py:370
  46.2 1.3 %copy.8 = bf16[2,1024]{1,0:T(2,128)(2,1)} copy(bf16[2,1024]{1,0:T(2,128)(2,1)} %shard_map.64) | data formatting | bytes 8192

commit v5 on v4

--- a/solution.py
+++ b/solution.py
@@ -193,15 +193,14 @@
         rows = gath[DEEP * g:DEEP * g + DEEP, :, :, :D].reshape(ROWS, D)
         lin = jnp.dot(rows, turned[...], preferred_element_type=F32)
         part[g] = lin.astype(BF16).reshape(4, PART, 2 * H)
-        for xs in range(4):
+        for d in (2, 1, 3):
+            xs = lax.rem(x + d, 4)
             if g == 0:
                 @pl.when(xs > x)
                 def _():
                     pl.semaphore_wait(inx.at[xs], 1)
 
-            @pl.when(xs != x)
-            def _():
-                share(g, xs).start()
+            share(g, xs).start()
 
     lanes = lax.broadcasted_iota(jnp.int32, (PART, 128), 1)
     named = (lanes == e) | (lanes == e + EXPERTS)
@@ -302,9 +301,9 @@
     activate(3)
     c7[1] = cores(1, c6[1])
     c6[2] = product(2)
-    line(0, c7[0])
     c7[2] = cores(2, c6[2])
     c6[3] = product(3)
+    line(0, c7[0])
     cores2(3, c6[3])
     line(1, c7[1])
     line(2, c7[2])

time: 47.6 us -> 47.7 us (level)
  no operation moved by 1% of the time
where the time goes in v5:
time: 47.7 us; the launch traced here: 47.5 us
  Pallas kernels  46.2 us (97%)
  local copies, waits for them, and re-layouts  1.28 us (3%)
    pallas_call x1, Pallas kernels, shards(): pl.pallas_call(body, out_shape=jax.ShapeDtypeStruct((TOK, D), BF16), in_s...  46.2 us
    unnamed x1, local copies, waits for them, and re-layouts  1.28 us

profile of v5, /device:TPU:448, one launch (start us, length us, event | category | flops | bytes accessed | tf_op | source)
XLA Modules:
  0.0 47.5 jit_solution(16480805461075755459)
XLA Ops:
  0.0 46.2 %shard_map.64 = bf16[2,1024]{1,0:T(2,128)(2,1)} custom-call(bf16[2,1024]{1,0:T(2,128)(2,1)} %tokens_hbm.1, s32[2,8]{1,0:T(2,128)} %routing_hbm.1, f32[2,8]{1,0:T(2,128)} %combine_hbm.1, bf16[384,1024]{1,0:T(8,128)(2,1)} %gate_hbm.1, bf16[384,1024]{1,0:T(8,128)(2,1)} %up_hbm.1, bf16[384,1024]{1,0:T(8,128)(2,1)} %down_hbm.1), custom_call_target="tpu_custom_call" | custom-call | flops 603979776 | bytes 2400000 | tf_op jit(solution)/shard_map/pallas_call | solution.py:369
  46.3 1.3 %copy.8 = bf16[2,1024]{1,0:T(2,128)(2,1)} copy(bf16[2,1024]{1,0:T(2,128)(2,1)} %shard_map.64) | data formatting | bytes 8192
